TPU v7x, 32 devices: a whole 2x2x4 slice. The times are simulated.
32 devices in a mesh: ka: 8 (over y, x, core), pw: 4 (over z).
Axes of the slice: x: 2, y: 2, z: 4, core: 2. Of those that a mesh axis runs over, the one named last changes fastest.
Arguments:
- coeffs: bfloat16 [128, 2, 1536, 256], P('ka', None, 'pw'), may hold values from -2.5 to 2.5
- neighbour: int32 [128], P('ka'), may hold values from 0 to 127, as said below
- gshift: int32 [1536], replicated, may hold values from 0 to 1535, each once
Outputs:
- inner_products: float32 [256, 128, 2, 256], P('pw', 'ka')
Inputs may be any that keep to these rules, and one draw needn't show every extreme that they name: neighbour[k] lies in the slab of 16 k-points that starts 2 * 16 points after the start of the slab of k, counted cyclically over the 128 points; the neighbours of one slab's points are distinct. `gshift`: each row appears once.
All inputs are finite; a program needn't handle non-finite values.
Results may differ from a plain program's by a relative error of at most 0.0003.
Values may be sent and summed in bfloat16 or wider, within the bound.
A program may use at most 128 MiB of HBM per device.

v0:
```python
import jax
import jax.numpy as jnp
from jax import lax
from jax.sharding import PartitionSpec as P

SHIFT_DEV = 2


def passed_along(block, axis, distance):
    devices = range(lax.axis_size(axis))
    route = [((i - distance) % len(devices), i) for i in devices]
    return lax.ppermute(block, axis, route)


def band_major_rows(own_rows, partner_block):
    products_all = jnp.einsum(
        "mkcg,kdgn->mkcdn", own_rows, partner_block, preferred_element_type=jnp.float32
    )
    real_part = products_all[:, :, 0, 0] + products_all[:, :, 1, 1]
    imag_part = products_all[:, :, 0, 1] - products_all[:, :, 1, 0]
    return jnp.stack([real_part, imag_part], axis=2)


def on_device(coeffs, neighbour, gshift):
    slab_points = coeffs.shape[0]
    ka_count = lax.axis_size("ka")
    wrapped = lax.axis_index("ka") >= ka_count - SHIFT_DEV
    arrived = passed_along(coeffs, "ka", -SHIFT_DEV)
    local_order = neighbour % slab_points
    partner = jnp.take(arrived, local_order, axis=0)
    permuted = jnp.take(
        lax.all_to_all(partner, "pw", split_axis=0, concat_axis=2, tiled=True), gshift, axis=2
    )
    permuted_all = lax.all_to_all(permuted, "pw", split_axis=2, concat_axis=0, tiled=True)
    partner = jnp.where(wrapped, permuted_all, partner)
    band_major = jnp.transpose(coeffs, (3, 0, 1, 2))
    return lax.psum_scatter(
        band_major_rows(band_major, partner), "pw", scatter_dimension=0, tiled=True
    )


def solution(mesh):
    placed = (P("ka", None, "pw", None), P("ka"), P())
    return jax.shard_map(
        on_device, mesh=mesh, in_specs=placed, out_specs=P("pw", "ka", None, None), check_vma=False
    )
```

profile of v0, /device:TPU:0, one launch (start us, length us, event | category | flops | bytes accessed | tf_op | source)
XLA Modules:
  0.0 700.2 jit_solution(10478675612138319184)
XLA Ops:
  6.5 3.9 collective-permute-start
  10.4 0.7 compare_and_fusion.1
  11.1 134.4 %collective-permute-done = bf16[16,2,384,256]{3,2,1,0:T(8,128)(2,1)} collective-permute-done((bf16[16,2,384,256]{3,2,1,0:T(8,128)(2,1)}, bf16[16,2,384,256]{3,2,1,0:T(8,128)(2,1)}, u32[]{:S(2)}, u32[]{:S(2)}) %collective-permute-start) | collective-permute-done | bytes 6291488 | tf_op jit(solution)/shard_map/ppermute | solution.py:12
  145.5 6.4 gather_fusion
  151.9 6.0 broadcast_select_fusion
  157.9 0.0 copy-start
  158.0 5.4 all-to-all-start
  163.3 0.0 copy-done
  163.4 137.6 %all-to-all-done = bf16[16,2,384,256]{3,2,1,0:T(8,128)(2,1)} async-done(((bf16[16,2,384,256]{3,2,1,0:T(8,128)(2,1)}), bf16[16,2,384,256]{3,2,1,0:T(8,128)(2,1)}, u32[]{:S(2)}, u32[]{:S(2)}) %all-to-all-start) | async-done | bytes 6291488 | tf_op jit(solution)/shard_map/all_to_all | solution.py:32
  301.0 3.2 copy.25
  304.2 25.2 %copy.26 = bf16[4,2,1536,256]{3,0,2,1:T(4,128)(2,1)} copy(bf16[4,2,1536,256]{3,2,1,0:T(8,128)(2,1)S(1)} %bitcast.41) | data formatting | bytes 12582912 | tf_op jit(solution)/shard_map/all_to_all | solution.py:32
  329.4 11.4 %gather_fusion.1 = bf16[1536,4,2,256]{3,1,2,0:T(4,128)(2,1)} fusion(bf16[4,2,1536,256]{3,0,2,1:T(4,128)(2,1)} %copy.26, s32[2048]{0:T(1024)S(1)} %pad_clamp_fusion), kind=kCustom, calls=%fused_computation.1 | custom fusion | bytes 12589056 | tf_op jit(solution)/shard_map/jit(_take)/gather | solution.py:31
  340.8 9.3 %select_bitcast_fusion = bf16[4,2,1536,256]{3,0,1,2:T(4,128)(2,1)} fusion(bf16[1536,4,2,256]{3,1,2,0:T(4,128)(2,1)} %gather_fusion.1, pred[1536]{0:T(1024)(128)(4,1)S(1)} %compare_and_fusion), kind=kLoop, calls=%fused_computation.7 | loop fusion | flops 3145728 | bytes 12584448 | tf_op jit(solution)/shard_map/jit(_take)/select_n | solution.py:31
  350.1 5.2 all-to-all-start.1
  355.4 0.2 reduce-scatter.2.cloned.1.call-start
  355.6 137.4 %all-to-all-done.1 = bf16[4,2,1536,256]{3,0,1,2:T(4,128)(2,1)} async-done(((bf16[4,2,1536,256]{3,0,1,2:T(4,128)(2,1)}), bf16[4,2,1536,256]{3,0,1,2:T(4,128)(2,1)}, u32[]{:S(2)}, u32[]{:S(2)}) %all-to-all-start.1) | async-done | bytes 6291488 | tf_op jit(solution)/shard_map/all_to_all | solution.py:34
  493.0 0.0 slice-start
  493.0 4.2 copy.27
  497.2 0.0 slice-start.1
  497.2 3.1 copy.28
  500.3 0.0 slice-done
  500.3 0.0 slice-done.1
  500.3 6.6 bitcast_select_fusion
  506.9 14.9 %convolution_bitcast_fusion = f32[256,16,2,2,256]{0,4,2,3,1:T(8,128)} fusion(bf16[16,2,384,256]{3,2,1,0:T(8,128)(2,1)} %param.3, bf16[16,2,384,256]{3,2,1,0:T(8,128)(2,1)} %bitcast_select_fusion), kind=kOutput, calls=%fused_computation.2 | convolution fusion | flops 3221225472 | bytes 29360128 | tf_op jit(solution)/shard_map/mkcg,kdgn->mkcdn/dot_general | solution.py:16
  521.8 4.0 fusion.2
  525.8 4.0 fusion.4
  529.9 3.8 pad_maximum_fusion
  533.7 10.3 %copy.33 = f32[256,16,2,256]{3,1,2,0:T(8,128)} copy(f32[256,16,2,256]{0,3,1,2:T(8,128)} %pad_maximum_fusion) | data formatting | bytes 16777216 | tf_op jit(solution)/shard_map/stack | solution.py:21
  544.0 0.0 reduce-scatter.2.cloned.1.call-update
  544.0 144.5 %reduce-scatter.2.cloned.1.call-done = f32[64,16,2,256]{3,1,2,0:T(8,128)} async-done(((f32[256,16,2,256]{3,1,2,0:T(8,128)}), f32[64,16,2,256]{3,1,2,0:T(8,128)}) %reduce-scatter.2.cloned.1.call-update) | async-done | bytes 2097168 | tf_op jit(solution)/shard_map/reduce_scatter | solution.py:37
  688.5 4.8 copy.34
  (5 shorter events, 0.0 us)
Async XLA Ops:
  6.5 139.0 %collective-permute-start = (bf16[16,2,384,256]{3,2,1,0:T(8,128)(2,1)}, bf16[16,2,384,256]{3,2,1,0:T(8,128)(2,1)}, u32[]{:S(2)}, u32[]{:S(2)}) collective-permute-start(bf16[16,2,384,256]{3,2,1,0:T(8,128)(2,1)} %param.3), channel_id=1, source_target_pairs={{8,0},{12,4},{16,8},{20,12},{24,16},{28,20},{0,24},{4,28},{9,1},{1... | collective-permute-start | bytes 18874376 | tf_op jit(solution)/shard_map/ppermute | solution.py:12
  157.9 5.4 copy-start
  158.0 143.0 %all-to-all-start = ((bf16[16,2,384,256]{3,2,1,0:T(8,128)(2,1)}), bf16[16,2,384,256]{3,2,1,0:T(8,128)(2,1)}, u32[]{:S(2)}, u32[]{:S(2)}) async-start(bf16[16,2,384,256]{3,2,1,0:T(8,128)(2,1)} %broadcast_select_fusion), calls=%async_computation | async-start | bytes 12582912 | tf_op jit(solution)/shard_map/all_to_all | solution.py:32
  350.1 142.9 %all-to-all-start.1 = ((bf16[4,2,1536,256]{3,0,1,2:T(4,128)(2,1)}), bf16[4,2,1536,256]{3,0,1,2:T(4,128)(2,1)}, u32[]{:S(2)}, u32[]{:S(2)}) async-start(bf16[4,2,1536,256]{3,0,1,2:T(4,128)(2,1)} %select_bitcast_fusion), calls=%async_computation.1 | async-start | bytes 12582912 | tf_op jit(solution)/shard_map/all_to_all | solution.py:34
  355.4 333.1 %reduce-scatter.2.cloned.1.call-start = ((), (), s32[]{:S(2)}) async-start(), calls=%async_computation.3 | async-start | bytes 10485760 | tf_op jit(solution)/shard_map/reduce_scatter | solution.py:37
  493.0 7.3 %slice-start = ((s8[6291456]{0:T(1024)(128)(4,1)}), s8[4194304]{0:T(1024)(128)(4,1)S(1)}, s32[]{:S(2)}) async-start(s8[6291456]{0:T(1024)(128)(4,1)} %bitcast.39), calls=%async_computation.4 | async-start | bytes 8388608
  497.2 3.1 slice-start.1
Sparse Core Ops, SparseCore 0:
  544.1 144.3 reduce-scatter.1
where the time goes:
time: 701 us; the launch traced here: 700 us
  waiting for transfers between devices  554 us (79%)
  local copies, waits for them, and re-layouts  68.7 us (10%)
  other arithmetic  34.4 us (5%)
  matrix products  14.9 us (2%)
  starting transfers between devices  14.7 us (2%)
  between operations  13.5 us (2%)
    reduce_scatter x1, waiting for transfers between devices, on_device(): lax.psum_scatter(band_major_rows(band_major, partner), 'pw', scatter_dime...  145 us
    all_to_all x1, waiting for transfers between devices, on_device(): lax.all_to_all(partner, 'pw', split_axis=0, concat_axis=2, tiled=True)  138 us
    all_to_all x1, waiting for transfers between devices, on_device(): lax.all_to_all(permuted, 'pw', split_axis=2, concat_axis=0, tiled=True)  137 us
    ppermute x1, waiting for transfers between devices, passed_along(): return lax.ppermute(block, axis, route)  134 us
    all_to_all x2, local copies, waits for them, and re-layouts, on_device(): lax.all_to_all(partner, 'pw', split_axis=0, concat_axis=2, tiled=True)  28.4 us
    dot_general x1, matrix products, band_major_rows(): jnp.einsum('mkcg,kdgn->mkcdn', own_rows, partner_block, preferred_element...  14.9 us
  transfers between devices with their start and end apart: 4, of which 4 were waited for; matrix products, arithmetic and copies ran while one was open for 0% of the time, Pallas kernels for 0%

commit v1 on v0

v1 whole, which is shorter than its diff:
```python
import functools

import jax
import jax.numpy as jnp
from jax import lax
from jax.experimental import pallas as pl
from jax.experimental.pallas import tpu as pltpu
from jax.sharding import PartitionSpec as P

SHIFT_DEV = 2
GROUP = 2
MESH = pl.DeviceIdType.MESH
SENT = jnp.float32


def contract(a, b):
    return lax.dot_general(a, b, (((0,), (0,)), ((), ())), preferred_element_type=jnp.float32)


def kernel(n_ka, n_pw, inv_ref, gshift_ref, x_ref, out_ref, y, own_k, sorted_own, sent, got, part, moved,
           y_send, y_recv, k_send, k_recv, p_send, p_recv):
    slab, _, rows, bands = x_ref.shape
    per_pw = slab // n_pw
    groups = slab // GROUP
    cut = bands // n_pw
    ka, pw = lax.axis_index("ka"), lax.axis_index("pw")
    source = lax.rem(ka + SHIFT_DEV, n_ka)
    target = lax.rem(ka + n_ka - SHIFT_DEV, n_ka)
    wrapped = ka >= n_ka - SHIFT_DEV
    feeds_wrapped = ka < SHIFT_DEV

    def peer(d):
        return lax.rem(pw + d, n_pw)

    barrier = pltpu.get_barrier_semaphore()

    @pl.loop(1, n_pw)
    def _(d):
        pl.semaphore_signal(barrier, inc=1, device_id=(ka, peer(d)), device_id_type=MESH)

    @pl.when(wrapped)
    def _():
        @pl.loop(0, n_pw)
        def _(d):
            pl.semaphore_signal(barrier, inc=1, device_id=(source, peer(d)), device_id_type=MESH)

    @pl.when(jnp.logical_not(wrapped))
    def _():
        pl.semaphore_signal(barrier, inc=1, device_id=(source, pw), device_id_type=MESH)

    @pl.when(feeds_wrapped)
    def _():
        pl.semaphore_wait(barrier, 2 * n_pw - 1)

    @pl.when(jnp.logical_not(feeds_wrapped))
    def _():
        pl.semaphore_wait(barrier, n_pw)

    def shift_plain(k):
        return pltpu.make_async_remote_copy(
            src_ref=x_ref.at[k], dst_ref=y.at[k], send_sem=y_send.at[k], recv_sem=y_recv.at[k],
            device_id=(target, pw), device_id_type=MESH)

    def shift_to_wrapped(kk, d):
        k = peer(d) * per_pw + kk
        slot = pw * per_pw + kk
        return pltpu.make_async_remote_copy(
            src_ref=x_ref.at[k], dst_ref=y.at[slot], send_sem=y_send.at[k], recv_sem=y_recv.at[slot],
            device_id=(target, peer(d)), device_id_type=MESH)

    def own_to_peer(kk, d):
        k = peer(d) * per_pw + kk
        slot = pw * per_pw + kk
        return pltpu.make_async_remote_copy(
            src_ref=sorted_own.at[k], dst_ref=own_k.at[slot], send_sem=k_send.at[k], recv_sem=k_recv.at[slot],
            device_id=(ka, peer(d)), device_id_type=MESH)

    def part_to_peer(g, d):
        return pltpu.make_async_remote_copy(
            src_ref=sent.at[pl.ds(g * GROUP, GROUP), :, pl.ds(pl.multiple_of(peer(d) * cut, cut), cut), :],
            dst_ref=got.at[pw, pl.ds(g * GROUP, GROUP)],
            send_sem=p_send.at[g, peer(d)], recv_sem=p_recv.at[g, pw],
            device_id=(ka, peer(d)), device_id_type=MESH)

    def part_from_peer(g, d):
        return pltpu.make_async_remote_copy(
            src_ref=sent.at[pl.ds(g * GROUP, GROUP), :, pl.ds(pl.multiple_of(peer(d) * cut, cut), cut), :],
            dst_ref=got.at[peer(d), pl.ds(g * GROUP, GROUP)],
            send_sem=p_send.at[g, peer(d)], recv_sem=p_recv.at[g, peer(d)],
            device_id=(ka, peer(d)), device_id_type=MESH)

    def whole_to_peer(kk, d):
        k = pw * per_pw + kk
        return pltpu.make_async_remote_copy(
            src_ref=sent.at[k, :, pl.ds(pl.multiple_of(peer(d) * cut, cut), cut), :],
            dst_ref=got.at[pw, k],
            send_sem=p_send.at[kk, peer(d)], recv_sem=p_recv.at[kk, pw],
            device_id=(ka, peer(d)), device_id_type=MESH)

    def whole_from_peer(kk, d):
        k = peer(d) * per_pw + kk
        return pltpu.make_async_remote_copy(
            src_ref=sent.at[k, :, pl.ds(pl.multiple_of(peer(d) * cut, cut), cut), :],
            dst_ref=got.at[peer(d), k],
            send_sem=p_send.at[kk, peer(d)], recv_sem=p_recv.at[kk, peer(d)],
            device_id=(ka, peer(d)), device_id_type=MESH)

    @pl.when(feeds_wrapped)
    def _():
        @pl.loop(0, per_pw)
        def _(kk):
            @pl.loop(0, n_pw)
            def _(d):
                shift_to_wrapped(kk, d).start()

    @pl.when(jnp.logical_not(feeds_wrapped))
    def _():
        @pl.loop(0, slab)
        def _(k):
            shift_plain(k).start()

    def keep(k):
        sent[k] = part[...].astype(SENT)
        out_ref[k] = part[:, pl.ds(pl.multiple_of(pw * cut, cut), cut), :]

    @pl.when(jnp.logical_not(wrapped))
    def _():
        @pl.loop(0, groups)
        def _(g):
            @pl.loop(0, GROUP)
            def _(kk):
                k = g * GROUP + kk
                pltpu.make_async_remote_copy(
                    src_ref=x_ref.at[k], dst_ref=y.at[k], send_sem=y_send.at[k], recv_sem=y_recv.at[k],
                    device_id=(target, pw), device_id_type=MESH).wait_recv()
                mine = x_ref[inv_ref[k]]
                other = y[k]
                part[0] = contract(mine.reshape(2 * rows, bands), other.reshape(2 * rows, bands))
                part[1] = contract(mine[0], other[1]) - contract(mine[1], other[0])
                keep(k)

            @pl.loop(1, n_pw)
            def _(d):
                part_to_peer(g, d).start()

        @pl.loop(0, groups)
        def _(g):
            @pl.loop(1, n_pw)
            def _(d):
                part_from_peer(g, d).wait_recv()
                span = pl.ds(g * GROUP, GROUP)
                out_ref[span] = out_ref[span] + got[peer(d), span].astype(jnp.float32)

        @pl.loop(0, groups)
        def _(g):
            @pl.loop(1, n_pw)
            def _(d):
                part_to_peer(g, d).wait_send()

    @pl.when(wrapped)
    def _():
        @pl.loop(0, per_pw)
        def _(kk):
            own_k[pw * per_pw + kk] = x_ref[inv_ref[pw * per_pw + kk]]

            @pl.loop(1, n_pw)
            def _(d):
                k = peer(d) * per_pw + kk
                sorted_own[k] = x_ref[inv_ref[k]]
                own_to_peer(kk, d).start()

        @pl.loop(0, per_pw)
        def _(kk):
            @pl.loop(0, n_pw)
            def _(s):
                slot = s * per_pw + kk
                pltpu.make_async_remote_copy(
                    src_ref=x_ref.at[slot], dst_ref=y.at[slot], send_sem=y_send.at[slot], recv_sem=y_recv.at[slot],
                    device_id=(target, pw), device_id_type=MESH).wait_recv()

            @pl.loop(1, n_pw)
            def _(d):
                slot = peer(d) * per_pw + kk
                pltpu.make_async_remote_copy(
                    src_ref=sorted_own.at[slot], dst_ref=own_k.at[slot], send_sem=k_send.at[slot],
                    recv_sem=k_recv.at[slot], device_id=(ka, peer(d)), device_id_type=MESH).wait_recv()

            part[...] = jnp.zeros_like(part)

            @pl.loop(0, n_pw)
            def _(i):
                wanted = gshift_ref[pl.ds(pl.multiple_of(i * rows, rows), rows), :]
                moved[...] = jnp.zeros_like(moved)

                @pl.loop(0, n_pw)
                def _(s):
                    place = lax.broadcasted_iota(jnp.int32, (rows, rows), 1) + s * rows
                    chosen = jnp.where(place == wanted, 1.0, 0.0).astype(jnp.bfloat16)
                    for c in range(2):
                        moved[c] += jnp.dot(chosen, y[s * per_pw + kk, c], preferred_element_type=jnp.float32)

                mine = own_k[i * per_pw + kk]
                other = moved[...].astype(jnp.bfloat16)
                part[0] += contract(mine.reshape(2 * rows, bands), other.reshape(2 * rows, bands))
                part[1] += contract(mine[0], other[1]) - contract(mine[1], other[0])

            keep(pw * per_pw + kk)

            @pl.loop(1, n_pw)
            def _(d):
                whole_to_peer(kk, d).start()

        @pl.loop(0, per_pw)
        def _(kk):
            @pl.loop(1, n_pw)
            def _(d):
                whole_from_peer(kk, d).wait_recv()
                k = peer(d) * per_pw + kk
                out_ref[k] = got[peer(d), k].astype(jnp.float32)

        @pl.loop(0, per_pw)
        def _(kk):
            @pl.loop(1, n_pw)
            def _(d):
                whole_to_peer(kk, d).wait_send()
                own_to_peer(kk, d).wait_send()

    @pl.when(feeds_wrapped)
    def _():
        @pl.loop(0, per_pw)
        def _(kk):
            @pl.loop(0, n_pw)
            def _(d):
                shift_to_wrapped(kk, d).wait_send()

    @pl.when(jnp.logical_not(feeds_wrapped))
    def _():
        @pl.loop(0, slab)
        def _(k):
            shift_plain(k).wait_send()


def on_device(n_ka, n_pw, coeffs, neighbour, gshift):
    slab, parts, rows, bands = coeffs.shape
    cut = bands // n_pw
    points = jnp.arange(slab, dtype=jnp.int32)
    local_order = neighbour % slab
    inverse = jnp.sum(jnp.where(local_order[:, None] == points[None, :], points[:, None], 0), axis=0)
    vmem = pl.BlockSpec(memory_space=pltpu.VMEM)
    flops = 8 * slab * rows * bands * bands
    summed = pl.pallas_call(
        functools.partial(kernel, n_ka, n_pw),
        out_shape=jax.ShapeDtypeStruct((slab, parts, cut, bands), jnp.float32),
        in_specs=[pl.BlockSpec(memory_space=pltpu.SMEM), vmem, vmem],
        out_specs=vmem,
        scratch_shapes=[
            pltpu.VMEM(coeffs.shape, coeffs.dtype),
            pltpu.VMEM(coeffs.shape, coeffs.dtype),
            pltpu.VMEM(coeffs.shape, coeffs.dtype),
            pltpu.VMEM((slab, parts, bands, bands), SENT),
            pltpu.VMEM((n_pw, slab, parts, cut, bands), SENT),
            pltpu.VMEM((parts, bands, bands), jnp.float32),
            pltpu.VMEM((parts, rows, bands), jnp.float32),
            pltpu.SemaphoreType.DMA((slab,)),
            pltpu.SemaphoreType.DMA((slab,)),
            pltpu.SemaphoreType.DMA((slab,)),
            pltpu.SemaphoreType.DMA((slab,)),
            pltpu.SemaphoreType.DMA((slab // GROUP, n_pw)),
            pltpu.SemaphoreType.DMA((slab // GROUP, n_pw)),
        ],
        compiler_params=pltpu.CompilerParams(
            collective_id=0, has_side_effects=True, vmem_limit_bytes=58 * 1024 * 1024),
        cost_estimate=pl.CostEstimate(flops=flops, bytes_accessed=3 * coeffs.size, transcendentals=0),
    )(inverse, gshift[:, None], coeffs)
    return jnp.transpose(jnp.take(summed, local_order, axis=0), (2, 0, 1, 3))


def solution(mesh):
    placed = (P("ka", None, "pw", None), P("ka"), P())
    return jax.shard_map(
        functools.partial(on_device, mesh.shape["ka"], mesh.shape["pw"]), mesh=mesh, in_specs=placed,
        out_specs=P("pw", "ka", None, None), check_vma=False
    )
```

time: 701 us -> 336 us (0.48)
  waiting for transfers between devices: 554 us -> 0 us
  Pallas kernels: 0 us -> 323 us
  local copies, waits for them, and re-layouts: 68.7 us -> 7.06 us
  other arithmetic: 34.4 us -> 1.62 us
  matrix products: 14.9 us -> 0 us
  starting transfers between devices: 14.7 us -> 0 us
  between operations: 13.5 us -> 0.03 us
    pallas_call x0 -> x1, Pallas kernels: none -> 323 us  [on_device(): pl.pallas_call(functools.partial(kernel, n_ka, n_pw), out_shape=jax.Shape...]
    all_to_all x2 -> x0, waiting for transfers between devices: 275 us -> none  [the longest x1 138 us: on_device(): lax.all_to_all(partner, 'pw', split_axis=0, concat_axis=2, tiled=True)]
    reduce_scatter x1 -> x0, waiting for transfers between devices: 145 us -> none  [on_device(): lax.psum_scatter(band_major_rows(band_major, partner), 'pw', scatter_dime...]
    ppermute x1 -> x0, waiting for transfers between devices: 134 us -> none  [passed_along(): return lax.ppermute(block, axis, route)]
    all_to_all x4 -> x0, local copies, waits for them, and re-layouts: 35.7 us -> none  [the longest x2 28.4 us: on_device(): lax.all_to_all(partner, 'pw', split_axis=0, concat_axis=2, tiled=True)]
    select_n x4 -> x2, other arithmetic: 21.9 us -> 0.34 us  [on_device(): return jnp.transpose(jnp.take(summed, local_order, axis=0), (2, 0, 1, 3))]
    gather x2 -> x1, local copies, waits for them, and re-layouts: 17.8 us -> 2.27 us  [on_device(): return jnp.transpose(jnp.take(summed, local_order, axis=0), (2, 0, 1, 3))]
    dot_general x1 -> x0, matrix products: 14.9 us -> none  [band_major_rows(): jnp.einsum('mkcg,kdgn->mkcdn', own_rows, partner_block, preferred_element...]
  transfers between devices with their start and end apart: 4 -> 0, of which waited for: 4 -> 0; matrix products, arithmetic and copies ran while one was open for 0% -> 0% of each run, Pallas kernels for 0% -> 0%
where the time goes in v1:
time: 336 us; the launch traced here: 332 us
  Pallas kernels  323 us (96%)
  local copies, waits for them, and re-layouts  7.06 us (2%)
    pallas_call x1, Pallas kernels, on_device(): pl.pallas_call(functools.partial(kernel, n_ka, n_pw), out_shape=jax.Shape...  323 us

profile of v1, /device:TPU:0, one launch (start us, length us, event | category | flops | bytes accessed | tf_op | source)
XLA Modules:
  0.0 332.2 jit_solution(8912615587126426625)
XLA Ops:
  0.0 0.7 compare_and_fusion
  0.7 0.6 select_reduce_fusion.inv_ref
  1.3 1.8 broadcast_in_dim.36.gshift_ref
  3.1 323.5 %shard_map.37 = f32[16,2,64,256]{3,2,1,0:T(8,128)} custom-call(s32[16]{0:T(128)} %select_reduce_fusion.inv_ref, s32[1536,1]{1,0:T(8,128)} %broadcast_in_dim.36.gshift_ref, bf16[16,2,384,256]{3,2,1,0:T(8,128)(2,1)} %x_ref.1), custom_call_target="tpu_custom_call" | custom-call | flops 3221225472 | bytes 9437184 | tf_op jit(solution)/shard_map/pallas_call | solution.py:251
  326.6 2.3 gather_fusion
  328.9 0.3 select_bitcast_fusion
  329.3 2.9 copy.8
  (2 shorter events, 0.0 us)

commit v2 on v1

--- a/solution.py
+++ b/solution.py
@@ -8,7 +8,6 @@
 from jax.sharding import PartitionSpec as P
 
 SHIFT_DEV = 2
-GROUP = 2
 MESH = pl.DeviceIdType.MESH
 SENT = jnp.float32
 
@@ -21,13 +20,15 @@
            y_send, y_recv, k_send, k_recv, p_send, p_recv):
     slab, _, rows, bands = x_ref.shape
     per_pw = slab // n_pw
-    groups = slab // GROUP
     cut = bands // n_pw
     ka, pw = lax.axis_index("ka"), lax.axis_index("pw")
     source = lax.rem(ka + SHIFT_DEV, n_ka)
     target = lax.rem(ka + n_ka - SHIFT_DEV, n_ka)
     wrapped = ka >= n_ka - SHIFT_DEV
-    feeds_wrapped = ka < SHIFT_DEV
+    relay = n_ka - SHIFT_DEV - 1
+    feeds_wrapped = ka == 0
+    feeds_relay = ka == 1
+    is_relay = ka == relay
 
     def peer(d):
         return lax.rem(pw + d, n_pw)
@@ -38,21 +39,35 @@
     def _(d):
         pl.semaphore_signal(barrier, inc=1, device_id=(ka, peer(d)), device_id_type=MESH)
 
-    @pl.when(wrapped)
+    def greet(other_ka, other_pw):
+        pl.semaphore_signal(barrier, inc=1, device_id=(other_ka, other_pw), device_id_type=MESH)
+
+    @pl.when(ka == n_ka - 2)
     def _():
         @pl.loop(0, n_pw)
         def _(d):
-            pl.semaphore_signal(barrier, inc=1, device_id=(source, peer(d)), device_id_type=MESH)
+            greet(0, peer(d))
+
+    @pl.when(ka == n_ka - 1)
+    def _():
+        @pl.loop(0, n_pw)
+        def _(d):
+            greet(relay, peer(d))
 
     @pl.when(jnp.logical_not(wrapped))
     def _():
-        pl.semaphore_signal(barrier, inc=1, device_id=(source, pw), device_id_type=MESH)
+        greet(source, pw)
+
+    @pl.when(is_relay)
+    def _():
+        greet(1, pw)
+        pl.semaphore_wait(barrier, 2 * n_pw)
 
     @pl.when(feeds_wrapped)
     def _():
         pl.semaphore_wait(barrier, 2 * n_pw - 1)
 
-    @pl.when(jnp.logical_not(feeds_wrapped))
+    @pl.when(jnp.logical_not(jnp.logical_or(feeds_wrapped, is_relay)))
     def _():
         pl.semaphore_wait(barrier, n_pw)
 
@@ -75,19 +90,44 @@
             src_ref=sorted_own.at[k], dst_ref=own_k.at[slot], send_sem=k_send.at[k], recv_sem=k_recv.at[slot],
             device_id=(ka, peer(d)), device_id_type=MESH)
 
-    def part_to_peer(g, d):
-        return pltpu.make_async_remote_copy(
-            src_ref=sent.at[pl.ds(g * GROUP, GROUP), :, pl.ds(pl.multiple_of(peer(d) * cut, cut), cut), :],
-            dst_ref=got.at[pw, pl.ds(g * GROUP, GROUP)],
-            send_sem=p_send.at[g, peer(d)], recv_sem=p_recv.at[g, pw],
-            device_id=(ka, peer(d)), device_id_type=MESH)
-
-    def part_from_peer(g, d):
-        return pltpu.make_async_remote_copy(
-            src_ref=sent.at[pl.ds(g * GROUP, GROUP), :, pl.ds(pl.multiple_of(peer(d) * cut, cut), cut), :],
-            dst_ref=got.at[peer(d), pl.ds(g * GROUP, GROUP)],
-            send_sem=p_send.at[g, peer(d)], recv_sem=p_recv.at[g, peer(d)],
-            device_id=(ka, peer(d)), device_id_type=MESH)
+    def shift_to_relay(k):
+        return pltpu.make_async_remote_copy(
+            src_ref=x_ref.at[k], dst_ref=own_k.at[k], send_sem=y_send.at[k], recv_sem=k_recv.at[k],
+            device_id=(relay, pw), device_id_type=MESH)
+
+    def relay_onward(kk, d):
+        k = peer(d) * per_pw + kk
+        slot = pw * per_pw + kk
+        return pltpu.make_async_remote_copy(
+            src_ref=own_k.at[k], dst_ref=y.at[slot], send_sem=k_send.at[k], recv_sem=y_recv.at[slot],
+            device_id=(n_ka - 1, peer(d)), device_id_type=MESH)
+
+    def piece(j):
+        return pl.ds(pl.multiple_of(j * cut, cut), cut)
+
+    def sum_onward(k, j, slot, to):
+        return pltpu.make_async_remote_copy(
+            src_ref=sent.at[k, :, piece(j), :], dst_ref=got.at[slot, k],
+            send_sem=p_send.at[k, j], recv_sem=p_recv.at[k, slot],
+            device_id=(ka, to), device_id_type=MESH)
+
+    right, left = lax.rem(pw + 1, n_pw), lax.rem(pw + n_pw - 1, n_pw)
+
+    def send_right(k, j):
+        sum_onward(k, j, j, right).start()
+
+    def send_left(k, j):
+        @pl.when(j == pw - 1)
+        def _():
+            sum_onward(k, j, n_pw, left).start()
+
+        @pl.when(j < pw - 1)
+        def _():
+            sum_onward(k, j, j, left).start()
+
+    def add_arrived(k, j):
+        sum_onward(k, j, j, right).wait_recv()
+        sent[k, :, piece(j), :] = sent[k, :, piece(j), :] + got[j, k]
 
     def whole_to_peer(kk, d):
         k = pw * per_pw + kk
@@ -113,7 +153,15 @@
             def _(d):
                 shift_to_wrapped(kk, d).start()
 
-    @pl.when(jnp.logical_not(feeds_wrapped))
+    @pl.when(feeds_relay)
+    def _():
+        @pl.loop(0, per_pw)
+        def _(kk):
+            @pl.loop(0, n_pw)
+            def _(d):
+                shift_to_relay(peer(d) * per_pw + kk).start()
+
+    @pl.when(ka >= 2)
     def _():
         @pl.loop(0, slab)
         def _(k):
@@ -125,37 +173,78 @@
 
     @pl.when(jnp.logical_not(wrapped))
     def _():
-        @pl.loop(0, groups)
-        def _(g):
-            @pl.loop(0, GROUP)
-            def _(kk):
-                k = g * GROUP + kk
-                pltpu.make_async_remote_copy(
-                    src_ref=x_ref.at[k], dst_ref=y.at[k], send_sem=y_send.at[k], recv_sem=y_recv.at[k],
-                    device_id=(target, pw), device_id_type=MESH).wait_recv()
+        @pl.loop(0, slab + 1)
+        def _(step):
+            @pl.when(step < slab)
+            def _():
+                k = step
+
+                @pl.when(is_relay)
+                def _():
+                    kk, d = k // n_pw, lax.rem(k, n_pw)
+                    shift_to_relay(peer(d) * per_pw + kk).wait_recv()
+                    relay_onward(kk, d).start()
+
+                shift_plain(k).wait_recv()
                 mine = x_ref[inv_ref[k]]
                 other = y[k]
                 part[0] = contract(mine.reshape(2 * rows, bands), other.reshape(2 * rows, bands))
                 part[1] = contract(mine[0], other[1]) - contract(mine[1], other[0])
                 keep(k)
 
-            @pl.loop(1, n_pw)
-            def _(d):
-                part_to_peer(g, d).start()
-
-        @pl.loop(0, groups)
-        def _(g):
-            @pl.loop(1, n_pw)
-            def _(d):
-                part_from_peer(g, d).wait_recv()
-                span = pl.ds(g * GROUP, GROUP)
-                out_ref[span] = out_ref[span] + got[peer(d), span].astype(jnp.float32)
-
-        @pl.loop(0, groups)
-        def _(g):
-            @pl.loop(1, n_pw)
-            def _(d):
-                part_to_peer(g, d).wait_send()
+                @pl.when(pw == 0)
+                def _():
+                    @pl.loop(1, n_pw)
+                    def _(i):
+                        send_right(k, n_pw - i)
+
+                @pl.when(pw == n_pw - 1)
+                def _():
+                    @pl.loop(0, n_pw - 1)
+                    def _(j):
+                        send_left(k, j)
+
+            @pl.when(step > 0)
+            def _():
+                k = step - 1
+
+                @pl.loop(0, n_pw)
+                def _(j):
+                    @pl.when(jnp.logical_and(j > pw, pw > 0))
+                    def _():
+                        add_arrived(k, j)
+                        send_right(k, j)
+
+                    @pl.when(jnp.logical_and(j < pw, pw < n_pw - 1))
+                    def _():
+                        add_arrived(k, j)
+                        send_left(k, j)
+
+        @pl.loop(0, slab)
+        def _(k):
+            @pl.when(pw > 0)
+            def _():
+                sum_onward(k, pw, pw, right).wait_recv()
+                out_ref[k] = out_ref[k] + got[pw, k]
+
+            @pl.when(pw < n_pw - 1)
+            def _():
+                sum_onward(k, pw, n_pw, left).wait_recv()
+                out_ref[k] = out_ref[k] + got[n_pw, k]
+
+        @pl.loop(0, slab)
+        def _(k):
+            @pl.loop(1, n_pw)
+            def _(d):
+                sum_onward(k, peer(d), peer(d), right).wait_send()
+
+    @pl.when(is_relay)
+    def _():
+        @pl.loop(0, per_pw)
+        def _(kk):
+            @pl.loop(0, n_pw)
+            def _(d):
+                relay_onward(kk, d).wait_send()
 
     @pl.when(wrapped)
     def _():
@@ -233,7 +322,13 @@
             def _(d):
                 shift_to_wrapped(kk, d).wait_send()
 
-    @pl.when(jnp.logical_not(feeds_wrapped))
+    @pl.when(feeds_relay)
+    def _():
+        @pl.loop(0, slab)
+        def _(k):
+            shift_to_relay(k).wait_send()
+
+    @pl.when(ka >= 2)
     def _():
         @pl.loop(0, slab)
         def _(k):
@@ -258,15 +353,15 @@
             pltpu.VMEM(coeffs.shape, coeffs.dtype),
             pltpu.VMEM(coeffs.shape, coeffs.dtype),
             pltpu.VMEM((slab, parts, bands, bands), SENT),
-            pltpu.VMEM((n_pw, slab, parts, cut, bands), SENT),
+            pltpu.VMEM((n_pw + 1, slab, parts, cut, bands), SENT),
             pltpu.VMEM((parts, bands, bands), jnp.float32),
             pltpu.VMEM((parts, rows, bands), jnp.float32),
             pltpu.SemaphoreType.DMA((slab,)),
             pltpu.SemaphoreType.DMA((slab,)),
             pltpu.SemaphoreType.DMA((slab,)),
             pltpu.SemaphoreType.DMA((slab,)),
-            pltpu.SemaphoreType.DMA((slab // GROUP, n_pw)),
-            pltpu.SemaphoreType.DMA((slab // GROUP, n_pw)),
+            pltpu.SemaphoreType.DMA((slab, n_pw + 1)),
+            pltpu.SemaphoreType.DMA((slab, n_pw + 1)),
         ],
         compiler_params=pltpu.CompilerParams(
             collective_id=0, has_side_effects=True, vmem_limit_bytes=58 * 1024 * 1024),

time: 336 us -> 289 us (0.86)
  Pallas kernels: 323 us -> 278 us
    pallas_call x1, Pallas kernels: 323 us -> 278 us  [on_device(): pl.pallas_call(functools.partial(kernel, n_ka, n_pw), out_shape=jax.Shape...]
where the time goes in v2:
time: 289 us; the launch traced here: 287 us
  Pallas kernels  278 us (96%)
  local copies, waits for them, and re-layouts  7.06 us (2%)
    pallas_call x1, Pallas kernels, on_device(): pl.pallas_call(functools.partial(kernel, n_ka, n_pw), out_shape=jax.Shape...  278 us

profile of v2, /device:TPU:0, one launch (start us, length us, event | category | flops | bytes accessed | tf_op | source)
XLA Modules:
  0.0 287.0 jit_solution(5885764604961580411)
XLA Ops:
  0.0 0.7 compare_and_fusion
  0.7 0.6 select_reduce_fusion.inv_ref
  1.3 1.8 broadcast_in_dim.36.gshift_ref
  3.1 278.3 %shard_map.37 = f32[16,2,64,256]{3,2,1,0:T(8,128)} custom-call(s32[16]{0:T(128)} %select_reduce_fusion.inv_ref, s32[1536,1]{1,0:T(8,128)} %broadcast_in_dim.36.gshift_ref, bf16[16,2,384,256]{3,2,1,0:T(8,128)(2,1)} %x_ref.1), custom_call_target="tpu_custom_call" | custom-call | flops 3221225472 | bytes 9437184 | tf_op jit(solution)/shard_map/pallas_call | solution.py:346
  281.4 2.3 gather_fusion
  283.7 0.3 select_bitcast_fusion
  284.0 2.9 %copy.8 = f32[64,16,2,256]{3,2,1,0:T(2,128)} copy(f32[64,16,2,256]{3,0,2,1:T(8,128)S(1)} %select_bitcast_fusion) | data formatting | bytes 4194304 | tf_op jit(solution)/shard_map/jit(_take)/select_n | solution.py:370
  (2 shorter events, 0.0 us)
